TPU v7x, 128 devices: a whole 4x4x4 slice. The times are simulated.
128 devices in a mesh: span: 4 (over y_lo, core), ctx: 32 (over x, y_hi, z).
Axes of the slice: x: 4, y: 4 (y_hi: 2, y_lo: 2; y = y_hi * 2 + y_lo), z: 4, core: 2. Of those that a mesh axis runs over, the one named last changes fastest.
Arguments:
- queries: bfloat16 [4, 2304, 4096], P('span', 'ctx'), may hold values from -6 to 6
- key_rows: bfloat16 [4, 2304, 4096], P('span', 'ctx'), may hold values from -6 to 6
- value_rows: bfloat16 [4, 2304, 4096], P('span', 'ctx'), may hold values from -6 to 6
- noise_steps: int32 [4], replicated, may hold values from 0 to 999
- span_order: int32 [4], replicated, may hold values from 0 to 3999, as said below
- token_counts: int32 [4], replicated, may hold values from 576 to 2304, as said below
Outputs:
- attended: bfloat16 [4, 2304, 4096], P('span', 'ctx')
Inputs may be any that keep to these rules, and one draw needn't show every extreme that they name: `token_counts`: some span has exactly 2304 valid tokens and some other span exactly 576. `span_order`: the positions of the 4 spans are all distinct.
All inputs are finite; a program needn't handle non-finite values.
Results may differ from a plain program's by a relative error of at most 0.006.
Values may be sent and summed in bfloat16 or wider, within the bound.
No kernel may reach another device: no remote copies, remote signals or barrier semaphores. Data moves between devices by JAX's collectives and lax.ppermute only.
A program may use at most 64 MiB of HBM per device.

v0:
```python
import functools
import math

import jax
import jax.numpy as jnp
from jax import lax
from jax.experimental import pallas as pl
from jax.experimental.pallas import tpu as pltpu
from jax.sharding import PartitionSpec as P

HEADS = 32
HD = 128
SPANS = 4
KEY_BLOCK = 768
EDGE_ROWS = 128
QUERY_TILE = 144
GROUP = 4
PACK_HEADS = 16
ITEMS = 512
VMEM_BYTES = 48 * 1024 * 1024


def head_gates(noise_steps, head):
    freq = jnp.exp(-math.log(10000.0) * head.astype(jnp.float32) / HEADS)
    return 1.0 + 0.5 * jnp.sin(noise_steps.astype(jnp.float32) * freq)


def pack_kernel(turn_ref, q_ref, k_ref, v_ref, o_ref):
    piece = q_ref.shape[0] // 3
    turn = turn_ref[0]
    for head in range(PACK_HEADS):
        columns = slice(head * HD, (head + 1) * HD)
        q = q_ref[:, columns].astype(jnp.float32)
        pieces = [q[n * piece : (n + 1) * piece] for n in range(3)]
        sides = [ref[:, columns].astype(jnp.float32) for ref in (k_ref, v_ref)]
        for member in range(SPANS):
            which = (member + SPANS - 1 - turn) % SPANS
            chosen = jnp.where(which == 0, pieces[0], jnp.where(which == 1, pieces[1], pieces[2]))
            chunk = jnp.concatenate([sides[member % 2], chosen], axis=0)
            o_ref[member, head] = chunk.astype(o_ref.dtype)


def pack(turn, q, k, v):
    tok = q.shape[0]
    columns = pl.BlockSpec((tok, PACK_HEADS * HD), lambda n: (0, n))
    return pl.pallas_call(
        pack_kernel,
        grid=(HEADS // PACK_HEADS,),
        out_shape=jax.ShapeDtypeStruct((SPANS, HEADS, tok + tok // 3, HD), q.dtype),
        in_specs=[pl.BlockSpec(memory_space=pltpu.SMEM), columns, columns, columns],
        out_specs=pl.BlockSpec((SPANS, PACK_HEADS, tok + tok // 3, HD), lambda n: (0, n, 0, 0)),
        name="pack",
    )(turn, q, k, v)


def prepare_kernel(meta, incoming_ref, queries, items):
    tokens = queries.shape[0]
    piece = tokens // (3 * incoming_ref.shape[0] // SPANS)
    skipped = incoming_ref.shape[1] - piece
    span_tiles = tokens // SPANS // QUERY_TILE
    member = meta[2 * SPANS + 1]

    def item(tile, block, span, flag):
        return tile + (block << 8) + (span << 16) + (flag << 20)

    idle = item(SPANS * span_tiles, 0, 0, 1)
    at = jnp.int32(GROUP)
    for extra in range(GROUP):
        items[extra] = idle
    per_tile = SPANS * QUERY_TILE
    span_blocks = tokens // KEY_BLOCK
    blocks = [(meta[SPANS + e] + KEY_BLOCK - 1) // KEY_BLOCK for e in range(SPANS)]
    for c in range(SPANS):
        tiles = (meta[SPANS + c] + per_tile - 1) // per_tile
        seen = [jnp.where(meta[e] <= meta[c], blocks[e], 0) for e in range(SPANS)]

        def tile_items(t, at, c=c, seen=seen):
            start = at
            for e in range(SPANS):

                def block_item(b, at, e=e):
                    flag = jnp.where(at == start, 1, 0)
                    items[at] = item(c * span_tiles + t, e * span_blocks + b, c, flag)
                    return at + 1

                at = lax.fori_loop(0, seen[e], block_item, at)
            items[at - 1] = items[at - 1] + (2 << 20)
            return at

        at = lax.fori_loop(0, tiles, tile_items, at)
    for extra in range(4 * GROUP):
        items[at + extra] = idle
    items[ITEMS - 1] = at

    per_load = QUERY_TILE // (3 * piece)

    def gather_tile(t, carry):
        rows = []
        for n in range(per_load):
            for k in range(3):
                source = (t * per_load + n) * SPANS + (member + 1 + k) % SPANS
                rows.append(incoming_ref[source].astype(jnp.float32)[skipped:])
        here = pl.ds(pl.multiple_of(t * QUERY_TILE, 16), QUERY_TILE)
        queries[here, :] = jnp.concatenate(rows, axis=0).astype(queries.dtype)
        return carry

    lax.fori_loop(0, SPANS * span_tiles, gather_tile, 0)


def prepare(incoming, meta, tokens):
    smem, vmem = pl.BlockSpec(memory_space=pltpu.SMEM), pl.BlockSpec(memory_space=pltpu.VMEM)
    return pl.pallas_call(
        prepare_kernel,
        out_shape=(
            jax.ShapeDtypeStruct((tokens, HD), incoming.dtype),
            jax.ShapeDtypeStruct((ITEMS,), jnp.int32),
        ),
        in_specs=[smem, vmem],
        out_specs=(vmem, smem),
        compiler_params=pltpu.CompilerParams(vmem_limit_bytes=VMEM_BYTES),
        name="prepare",
    )(meta, incoming)


def attend_kernel(
    meta, gates, items, first_ref, second_ref, queries, o_ref,
    keys, values, scores, highs, weights, scales, acc, top, results, sems,
):
    chunks, piece = o_ref.shape[0], o_ref.shape[1]
    tokens = first_ref.shape[0] // SPANS
    all_tiles = tokens // QUERY_TILE
    core, member = meta[2 * SPANS], meta[2 * SPANS + 1]
    scale = math.log2(math.e) / math.sqrt(HD)

    def loads(key_src, value_src):
        return (
            pltpu.make_async_copy(key_src, keys, sems.at[0]),
            pltpu.make_async_copy(value_src, values.at[:, pl.ds(0, HD)], sems.at[1]),
        )

    @pl.when(core == 0)
    def _():
        for copy in loads(first_ref, second_ref):
            copy.start()

    @pl.when(core != 0)
    def _():
        for copy in loads(second_ref, first_ref):
            copy.start()

    values[:, HD:] = jnp.ones((values.shape[0], HD), values.dtype)
    for copy in loads(first_ref, second_ref):
        copy.wait()

    for e in range(SPANS):
        count = meta[SPANS + e]
        ends = (count + KEY_BLOCK - 1) // KEY_BLOCK * (KEY_BLOCK // EDGE_ROWS)
        first_key = keys[e * tokens : e * tokens + 16, :].astype(jnp.float32)[0:1, :]

        def edge(s, carry, e=e, count=count, first_key=first_key):
            rows = pl.ds(pl.multiple_of(e * tokens + s * EDGE_ROWS, EDGE_ROWS), EDGE_ROWS)
            left = count - s * EDGE_ROWS
            valid = lax.broadcasted_iota(jnp.int32, (EDGE_ROWS, HD), 0) < left
            block = keys[rows, :].astype(jnp.float32)
            keys[rows, :] = jnp.where(valid, block, first_key).astype(keys.dtype)
            for side in range(2):
                columns = slice(side * HD, (side + 1) * HD)
                mixed = values[rows, columns].astype(jnp.float32)
                values[rows, columns] = jnp.where(valid, mixed, 0.0).astype(values.dtype)
            return carry

        lax.fori_loop(count // EDGE_ROWS, ends, edge, 0)

    def key_rows(i):
        return pl.ds(pl.multiple_of((items[i] >> 8 & 255) * KEY_BLOCK, KEY_BLOCK), KEY_BLOCK)

    def parts_of(x):
        return [x[:, n * HD : (n + 1) * HD] for n in range(KEY_BLOCK // HD)]

    def score(i, at):
        tile = jnp.minimum(items[i] & 255, all_tiles - 1)
        q = queries[pl.ds(pl.multiple_of(tile * QUERY_TILE, 16), QUERY_TILE), :]
        x = lax.dot_general(
            q, keys[key_rows(i), :], (((1,), (1,)), ((), ())), preferred_element_type=jnp.float32
        )
        scores[at][...] = x
        highs[at][...] = functools.reduce(jnp.maximum, parts_of(x))

    def weigh(i, at):
        old = jnp.where((items[i] >> 20) & 1 == 1, -1e30, top[...])
        new = jnp.maximum(old, jnp.max(highs[at][...], axis=1, keepdims=True) * scale)
        top[...] = new
        scales[at][...] = jnp.exp2(old - new)
        for n, part in enumerate(parts_of(scores[at])):
            weight = jnp.exp2(part * scale - new)
            weights[at][:, n * HD : (n + 1) * HD] = weight.astype(jnp.bfloat16)

    def mix(i, at):
        mixed = jnp.dot(weights[at][...], values[key_rows(i), :], preferred_element_type=jnp.float32)
        factor = scales[at][...]
        sums = acc[:, :HD] * factor + mixed[:, :HD]
        totals = acc[:, HD:] * factor + mixed[:, HD:]
        acc[:, :HD] = sums
        acc[:, HD:] = totals
        rows = pl.ds(pl.multiple_of((items[i] & 255) * QUERY_TILE, 16), QUERY_TILE)
        results[rows, :] = sums * (gates[items[i] >> 16 & 3] / totals)

    acc[...] = jnp.ones(acc.shape, acc.dtype)
    top[...] = jnp.zeros(top.shape, top.dtype)
    for g in range(GROUP):
        weights[g][...] = jnp.ones(weights[g].shape, weights[g].dtype)
        scales[g][...] = jnp.zeros(scales[g].shape, scales[g].dtype)
        score(GROUP + g, GROUP + g)

    def two_steps(j, carry):
        for half in range(2):
            here, there = (half + 1) % 2 * GROUP, half * GROUP
            first = (2 * j + half) * GROUP
            for g in range(GROUP):
                score(first + 2 * GROUP + g, there + g)
            for g in range(GROUP):
                weigh(first + GROUP + g, here + g)
            for g in range(GROUP):
                mix(first + g, there + g)
        return carry

    lax.fori_loop(0, (items[ITEMS - 1] + 2 * GROUP - 1) // (2 * GROUP), two_steps, 0)

    def hand_back(t, carry):
        for k in range(3):
            rows = pl.ds(pl.multiple_of((t * 3 + k) * piece, 8), piece)
            o_ref[t * SPANS + (member + 1 + k) % SPANS] = results[rows, :].astype(o_ref.dtype)
        return carry

    lax.fori_loop(0, chunks // SPANS, hand_back, 0)


def attend(first, second, incoming, meta, gates):
    chunks = incoming.shape[0]
    piece = incoming.shape[1] - first.shape[0] // chunks
    tokens = first.shape[0] // SPANS
    queries, items = prepare(incoming, meta, tokens)
    smem, anywhere = pl.BlockSpec(memory_space=pltpu.SMEM), pl.BlockSpec(memory_space=pl.ANY)
    vmem = pl.BlockSpec(memory_space=pltpu.VMEM)
    tile, strip = (QUERY_TILE, KEY_BLOCK), (QUERY_TILE, HD)
    return pl.pallas_call(
        attend_kernel,
        out_shape=jax.ShapeDtypeStruct((chunks, piece, HD), first.dtype),
        in_specs=[smem, smem, smem, anywhere, anywhere, vmem],
        out_specs=vmem,
        scratch_shapes=[
            pltpu.VMEM(first.shape, first.dtype),
            pltpu.VMEM((first.shape[0], 2 * HD), first.dtype),
            [pltpu.VMEM(tile, jnp.float32)] * (2 * GROUP),
            [pltpu.VMEM(strip, jnp.float32)] * (2 * GROUP),
            [pltpu.VMEM(tile, jnp.bfloat16)] * (2 * GROUP),
            [pltpu.VMEM(strip, jnp.float32)] * (2 * GROUP),
            pltpu.VMEM((QUERY_TILE, 2 * HD), jnp.float32),
            pltpu.VMEM(strip, jnp.float32),
            pltpu.VMEM((tokens + QUERY_TILE, HD), jnp.float32),
            pltpu.SemaphoreType.DMA((2,)),
        ],
        compiler_params=pltpu.CompilerParams(vmem_limit_bytes=VMEM_BYTES),
        name="attend",
    )(meta, gates, items, first, second, queries)


def turned(x, axis, start, length):
    return lax.dynamic_slice_in_dim(jnp.concatenate([x, x], axis=axis), start, length, axis=axis)


def shards(queries, key_rows, value_rows, noise_steps, span_order, token_counts):
    both = ("span", "ctx")
    tok = queries.shape[1]
    piece = tok // 3
    ctx_size = lax.axis_size("ctx")
    me = lax.axis_index("span")
    place = lax.axis_index("ctx")
    turn = place % SPANS
    core = me % 2

    outgoing = pack(turn[None], queries[0], key_rows[0], value_rows[0])
    outgoing = outgoing.reshape(SPANS * HEADS, tok + piece, HD)
    incoming = lax.all_to_all(outgoing, both, split_axis=0, concat_axis=0, tiled=True)

    first = incoming[:, :tok].reshape(SPANS * ctx_size * tok, HD)
    second = lax.ppermute(first, "span", [(0, 1), (1, 0), (2, 3), (3, 2)])
    gates = head_gates(noise_steps, place)
    meta = jnp.concatenate([span_order, token_counts, core[None], me[None]]).astype(jnp.int32)
    out = attend(first, second, incoming, meta, gates)

    back = lax.all_to_all(out, both, split_axis=0, concat_axis=0, tiled=True)
    back = turned(back.reshape(SPANS, HEADS, piece, HD), 0, turn + 1, 3)
    back = back.transpose(0, 2, 1, 3).reshape(tok, HEADS * HD)
    token = place * tok + jnp.arange(tok)
    back = jnp.where((token < token_counts[me])[:, None], back, jnp.zeros((), back.dtype))
    return back[None]


def solution(mesh):
    tokens = P("span", "ctx", None)
    return jax.shard_map(
        shards,
        mesh=mesh,
        in_specs=(tokens, tokens, tokens, P(), P(), P()),
        out_specs=tokens,
        check_vma=False,
    )
```

profile of v0, /device:TPU:0, one launch (start us, length us, event | category | flops | bytes accessed | tf_op | source)
XLA Modules:
  0.0 103.5 jit_solution(10717687644600078200)
XLA Ops:
  0.0 3.0 %pack.1 = bf16[4,32,96,128]{3,2,1,0:T(8,128)(2,1)} custom-call(s32[1]{0:T(128)} %bitcast.3.turn_ref, bf16[72,4096]{1,0:T(8,128)(2,1)} %bitcast.16, bf16[72,4096]{1,0:T(8,128)(2,1)} %bitcast.17, bf16[72,4096]{1,0:T(8,128)(2,1)} %bitcast.18), custom_call_target="tpu_custom_call" | custom-call | tf_op jit(solution)/shard_map/pack/pallas_call | solution.py:46
  3.0 52.6 %all_to_all.10.incoming_ref = bf16[128,96,128]{2,1,0:T(8,128)(2,1)S(1)} all-to-all(bf16[128,96,128]{2,1,0:T(8,128)(2,1)} %bitcast.14), channel_id=1, replica_groups=mesh['span'=4,'ctx'=32] {'span','ctx'}, dimensions={0} | all-to-all | bytes 6291456 | tf_op jit(solution)/shard_map/all_to_all | solution.py:284
  55.6 0.0 copy-start
  55.6 0.0 copy-start.1
  55.6 0.0 copy-start.2
  55.7 1.6 %slice.4 = bf16[128,72,128]{2,1,0:T(8,128)(2,1)} slice(bf16[128,96,128]{2,1,0:T(8,128)(2,1)S(1)} %all_to_all.10.incoming_ref), slice={[0:128], [0:72], [0:128]} | slice | bytes 4718592 | tf_op jit(solution)/shard_map/slice | solution.py:286
  57.2 0.0 collective-permute-start
  57.3 0.0 copy-done
  57.3 0.0 copy-done.1
  57.3 0.1 pad_add_fusion.meta
  57.4 0.0 copy-done.2
  57.4 2.2 %prepare.1 = (bf16[2304,128]{1,0:T(8,128)(2,1)S(1)}, s32[512]{0:T(512)S(1)}) custom-call(s32[10]{0:T(128)S(1)} %pad_add_fusion.meta, bf16[128,96,128]{2,1,0:T(8,128)(2,1)S(1)} %all_to_all.10.incoming_ref), custom_call_target="tpu_custom_call" | custom-call | tf_op jit(solution)/shard_map/prepare/pallas_call | solution.py:112
  59.6 2.5 %collective-permute-done.second_ref = bf16[9216,128]{1,0:T(8,128)(2,1)} collective-permute-done((bf16[9216,128]{1,0:T(8,128)(2,1)}, bf16[9216,128]{1,0:T(8,128)(2,1)}, u32[]{:S(2)}, u32[]{:S(2)}) %collective-permute-start) | collective-permute-done | bytes 2359328 | tf_op jit(solution)/shard_map/ppermute | solution.py:287
  62.1 18.0 %attend.1 = bf16[128,24,128]{2,1,0:T(8,128)(2,1)} custom-call(s32[10]{0:T(128)S(1)} %pad_add_fusion.meta, f32[4]{0:T(128)S(1)} %multiply_add_fusion.gates, s32[512]{0:T(512)S(1)} %get-tuple-element.7.items, bf16[9216,128]{1,0:T(8,128)(2,1)} %bitcast.8.first_ref, bf16[9216,128]{1,0:T(8,128)(2,1)} %collective-permute-done.second_ref, ...), custom_call_target="tpu_custom_call" | custom-call | tf_op jit(solution)/shard_map/attend/pallas_call | solution.py:246
  80.1 5.5 %all-to-all-start.1 = ((bf16[128,24,128]{2,1,0:T(8,128)(2,1)}), bf16[128,24,128]{2,1,0:T(8,128)(2,1)S(1)}, u32[]{:S(2)}, u32[]{:S(2)}) async-start(bf16[128,24,128]{2,1,0:T(8,128)(2,1)} %attend.1), calls=%async_computation.1 | async-start | bytes 1572864 | tf_op jit(solution)/shard_map/all_to_all | solution.py:292
  85.7 0.6 dynamic_slice.6
  86.2 0.7 add_compare_fusion
  86.9 15.1 %all-to-all-done.1 = bf16[128,24,128]{2,1,0:T(8,128)(2,1)S(1)} async-done(((bf16[128,24,128]{2,1,0:T(8,128)(2,1)}), bf16[128,24,128]{2,1,0:T(8,128)(2,1)S(1)}, u32[]{:S(2)}, u32[]{:S(2)}) %all-to-all-start.1) | async-done | bytes 786464 | tf_op jit(solution)/shard_map/all_to_all | solution.py:292
  102.0 0.2 fusion.1
  102.2 0.1 copy.7
  102.3 0.3 reshape.49
  102.6 0.9 broadcast_select_fusion
  (1 shorter events, 0.0 us)
Async XLA Ops:
  55.6 1.7 %copy-start = (s32[4]{0:T(128)S(1)}, s32[4]{0:T(128)}, u32[]{:S(2)}) copy-start(s32[4]{0:T(128)} %param.10) | copy-start | bytes 52
  55.6 1.7 %copy-start.1 = (s32[4]{0:T(128)S(1)}, s32[4]{0:T(128)}, u32[]{:S(2)}) copy-start(s32[4]{0:T(128)} %param.11) | copy-start | bytes 52
  55.6 1.7 %copy-start.2 = (s32[4]{0:T(128)S(1)}, s32[4]{0:T(128)}, u32[]{:S(2)}) copy-start(s32[4]{0:T(128)} %param.9) | copy-start | bytes 52
  57.2 4.9 %collective-permute-start = (bf16[9216,128]{1,0:T(8,128)(2,1)}, bf16[9216,128]{1,0:T(8,128)(2,1)}, u32[]{:S(2)}, u32[]{:S(2)}) collective-permute-start(bf16[9216,128]{1,0:T(8,128)(2,1)} %bitcast.8.first_ref), channel_id=1, source_target_pairs={{0,32},{32,0},{64,96},{96,64},{1,33},{33,1},{65,97},{97,65},{2,34}... | collective-permute-start | bytes 7077896 | tf_op jit(solution)/shard_map/ppermute | solution.py:287
  80.1 21.9 %all-to-all-start.1 = ((bf16[128,24,128]{2,1,0:T(8,128)(2,1)}), bf16[128,24,128]{2,1,0:T(8,128)(2,1)S(1)}, u32[]{:S(2)}, u32[]{:S(2)}) async-start(bf16[128,24,128]{2,1,0:T(8,128)(2,1)} %attend.1), calls=%async_computation.1 | async-start | bytes 1572864 | tf_op jit(solution)/shard_map/all_to_all | solution.py:292
where the time goes:
time: 103 us; the launch traced here: 104 us
  blocking collectives  52.6 us (51%)
  Pallas kernels  23.2 us (23%)
  waiting for transfers between devices  17.6 us (17%)
  starting transfers between devices  5.51 us (5%)
  local copies, waits for them, and re-layouts  2.53 us (2%)
  other arithmetic  1.91 us (2%)
    all_to_all x1, blocking collectives, shards(): lax.all_to_all(outgoing, both, split_axis=0, concat_axis=0, tiled=True)  52.6 us
    pallas_call x1, Pallas kernels, attend(): pl.pallas_call(attend_kernel, out_shape=jax.ShapeDtypeStruct((chunks, pie...  18 us
    all_to_all x1, waiting for transfers between devices, shards(): back = lax.all_to_all(out, both, split_axis=0, concat_axis=0, tiled=True)  15.1 us
    all_to_all x1, starting transfers between devices, shards(): back = lax.all_to_all(out, both, split_axis=0, concat_axis=0, tiled=True)  5.5 us
    pallas_call x1, Pallas kernels, pack(): pl.pallas_call(pack_kernel, grid=(HEADS // PACK_HEADS,), out_shape=jax.Sh...  3.01 us
    ppermute x1, waiting for transfers between devices, shards(): second = lax.ppermute(first, 'span', [(0, 1), (1, 0), (2, 3), (3, 2)])  2.47 us
    pallas_call x1, Pallas kernels, prepare(): pl.pallas_call(prepare_kernel, out_shape=(jax.ShapeDtypeStruct((tokens, H...  2.2 us
  transfers between devices with their start and end apart: 2, of which 2 were waited for; matrix products, arithmetic and copies ran while one was open for 1% of the time, Pallas kernels for 2%

commit v1 on v0

--- a/solution.py
+++ b/solution.py
@@ -15,9 +15,10 @@
 EDGE_ROWS = 128
 QUERY_TILE = 144
 GROUP = 4
-PACK_HEADS = 16
+PACK_HEADS = 8
 ITEMS = 512
-VMEM_BYTES = 48 * 1024 * 1024
+ATTEND_VMEM = 24 * 1024 * 1024
+PREPARE_VMEM = 8 * 1024 * 1024
 
 
 def head_gates(noise_steps, head):
@@ -25,30 +26,52 @@
     return 1.0 + 0.5 * jnp.sin(noise_steps.astype(jnp.float32) * freq)
 
 
-def pack_kernel(turn_ref, q_ref, k_ref, v_ref, o_ref):
-    piece = q_ref.shape[0] // 3
+def pack_kernel(turn_ref, q_hbm, k_hbm, v_hbm, packed, given, in_sems):
+    tok = q_hbm.shape[0]
+    piece = tok // 3
     turn = turn_ref[0]
-    for head in range(PACK_HEADS):
-        columns = slice(head * HD, (head + 1) * HD)
-        q = q_ref[:, columns].astype(jnp.float32)
-        pieces = [q[n * piece : (n + 1) * piece] for n in range(3)]
-        sides = [ref[:, columns].astype(jnp.float32) for ref in (k_ref, v_ref)]
-        for member in range(SPANS):
-            which = (member + SPANS - 1 - turn) % SPANS
-            chosen = jnp.where(which == 0, pieces[0], jnp.where(which == 1, pieces[1], pieces[2]))
-            chunk = jnp.concatenate([sides[member % 2], chosen], axis=0)
-            o_ref[member, head] = chunk.astype(o_ref.dtype)
+    steps = HEADS // PACK_HEADS
+
+    def arriving(n):
+        columns = pl.ds(n * PACK_HEADS * HD, PACK_HEADS * HD)
+        return [
+            pltpu.make_async_copy(ref.at[:, columns], given.at[side, :, columns], in_sems.at[side, n])
+            for side, ref in enumerate((k_hbm, v_hbm, q_hbm))
+        ]
+
+    for n in range(steps):
+        for copy in arriving(n):
+            copy.start()
+    for n in range(steps):
+        for copy in arriving(n):
+            copy.wait()
+        for head in range(n * PACK_HEADS, (n + 1) * PACK_HEADS):
+            columns = slice(head * HD, (head + 1) * HD)
+            sides = [given[side, :, columns].astype(jnp.float32) for side in range(3)]
+            pieces = [sides[2][m * piece : (m + 1) * piece] for m in range(3)]
+            for member in range(SPANS):
+                which = (member + SPANS - 1 - turn) % SPANS
+                chosen = jnp.where(
+                    which == 0, pieces[0], jnp.where(which == 1, pieces[1], pieces[2])
+                )
+                chunk = jnp.concatenate([sides[member % 2], chosen], axis=0)
+                packed[member, head] = chunk.astype(packed.dtype)
 
 
 def pack(turn, q, k, v):
     tok = q.shape[0]
-    columns = pl.BlockSpec((tok, PACK_HEADS * HD), lambda n: (0, n))
+    hbm = pl.BlockSpec(memory_space=pltpu.HBM)
+    q, k, v = (pltpu.with_memory_space_constraint(x, pltpu.HBM) for x in (q, k, v))
     return pl.pallas_call(
         pack_kernel,
-        grid=(HEADS // PACK_HEADS,),
-        out_shape=jax.ShapeDtypeStruct((SPANS, HEADS, tok + tok // 3, HD), q.dtype),
-        in_specs=[pl.BlockSpec(memory_space=pltpu.SMEM), columns, columns, columns],
-        out_specs=pl.BlockSpec((SPANS, PACK_HEADS, tok + tok // 3, HD), lambda n: (0, n, 0, 0)),
+        out_shape=pltpu.VMEM((SPANS, HEADS, tok + tok // 3, HD), q.dtype),
+        in_specs=[pl.BlockSpec(memory_space=pltpu.SMEM), hbm, hbm, hbm],
+        out_specs=pl.BlockSpec(memory_space=pltpu.VMEM),
+        scratch_shapes=[
+            pltpu.VMEM((3,) + q.shape, q.dtype),
+            pltpu.SemaphoreType.DMA((3, HEADS // PACK_HEADS)),
+        ],
+        compiler_params=pltpu.CompilerParams(vmem_limit_bytes=PREPARE_VMEM),
         name="pack",
     )(turn, q, k, v)
 
@@ -112,12 +135,12 @@
     return pl.pallas_call(
         prepare_kernel,
         out_shape=(
-            jax.ShapeDtypeStruct((tokens, HD), incoming.dtype),
+            pltpu.VMEM((tokens, HD), incoming.dtype),
             jax.ShapeDtypeStruct((ITEMS,), jnp.int32),
         ),
         in_specs=[smem, vmem],
         out_specs=(vmem, smem),
-        compiler_params=pltpu.CompilerParams(vmem_limit_bytes=VMEM_BYTES),
+        compiler_params=pltpu.CompilerParams(vmem_limit_bytes=PREPARE_VMEM),
         name="prepare",
     )(meta, incoming)
 
@@ -132,27 +155,32 @@
     core, member = meta[2 * SPANS], meta[2 * SPANS + 1]
     scale = math.log2(math.e) / math.sqrt(HD)
 
-    def loads(key_src, value_src):
+    def loads(key_src, value_src, e):
+        rows = pl.ds(e * tokens, tokens)
         return (
-            pltpu.make_async_copy(key_src, keys, sems.at[0]),
-            pltpu.make_async_copy(value_src, values.at[:, pl.ds(0, HD)], sems.at[1]),
+            pltpu.make_async_copy(key_src.at[rows], keys.at[rows], sems.at[0, e]),
+            pltpu.make_async_copy(
+                value_src.at[rows], values.at[rows, pl.ds(0, HD)], sems.at[1, e]
+            ),
         )
 
     @pl.when(core == 0)
     def _():
-        for copy in loads(first_ref, second_ref):
-            copy.start()
+        for e in range(SPANS):
+            for copy in loads(first_ref, second_ref, e):
+                copy.start()
 
     @pl.when(core != 0)
     def _():
-        for copy in loads(second_ref, first_ref):
-            copy.start()
+        for e in range(SPANS):
+            for copy in loads(second_ref, first_ref, e):
+                copy.start()
 
     values[:, HD:] = jnp.ones((values.shape[0], HD), values.dtype)
-    for copy in loads(first_ref, second_ref):
-        copy.wait()
 
     for e in range(SPANS):
+        for copy in loads(first_ref, second_ref, e):
+            copy.wait()
         count = meta[SPANS + e]
         ends = (count + KEY_BLOCK - 1) // KEY_BLOCK * (KEY_BLOCK // EDGE_ROWS)
         first_key = keys[e * tokens : e * tokens + 16, :].astype(jnp.float32)[0:1, :]
@@ -240,12 +268,14 @@
     piece = incoming.shape[1] - first.shape[0] // chunks
     tokens = first.shape[0] // SPANS
     queries, items = prepare(incoming, meta, tokens)
+    first = pltpu.with_memory_space_constraint(first, pltpu.VMEM)
+    second = pltpu.with_memory_space_constraint(second, pltpu.VMEM)
     smem, anywhere = pl.BlockSpec(memory_space=pltpu.SMEM), pl.BlockSpec(memory_space=pl.ANY)
     vmem = pl.BlockSpec(memory_space=pltpu.VMEM)
     tile, strip = (QUERY_TILE, KEY_BLOCK), (QUERY_TILE, HD)
     return pl.pallas_call(
         attend_kernel,
-        out_shape=jax.ShapeDtypeStruct((chunks, piece, HD), first.dtype),
+        out_shape=pltpu.VMEM((chunks, piece, HD), first.dtype),
         in_specs=[smem, smem, smem, anywhere, anywhere, vmem],
         out_specs=vmem,
         scratch_shapes=[
@@ -258,9 +288,9 @@
             pltpu.VMEM((QUERY_TILE, 2 * HD), jnp.float32),
             pltpu.VMEM(strip, jnp.float32),
             pltpu.VMEM((tokens + QUERY_TILE, HD), jnp.float32),
-            pltpu.SemaphoreType.DMA((2,)),
+            pltpu.SemaphoreType.DMA((2, SPANS)),
         ],
-        compiler_params=pltpu.CompilerParams(vmem_limit_bytes=VMEM_BYTES),
+        compiler_params=pltpu.CompilerParams(vmem_limit_bytes=ATTEND_VMEM),
         name="attend",
     )(meta, gates, items, first, second, queries)
 

time: 103 us -> 99.2 us (0.963); the launches traced: 104 us -> 97.4 us
  Pallas kernels: 23.2 us -> 17.2 us
    pallas_call x3, Pallas kernels: 23.2 us -> 17.2 us  [the longest x1 13.4 us: attend(): pl.pallas_call(attend_kernel, out_shape=pltpu.VMEM((chunks, piece, HD), f...]
where the time goes in v1:
time: 99.2 us; the launch traced here: 97.4 us
  blocking collectives  52.4 us (53%)
  waiting for transfers between devices  17.8 us (18%)
  Pallas kernels  17.2 us (17%)
  starting transfers between devices  5.51 us (6%)
  local copies, waits for them, and re-layouts  2.53 us (3%)
  other arithmetic  1.91 us (2%)
    all_to_all x1, blocking collectives, shards(): lax.all_to_all(outgoing, both, split_axis=0, concat_axis=0, tiled=True)  52.4 us
    all_to_all x1, waiting for transfers between devices, shards(): back = lax.all_to_all(out, both, split_axis=0, concat_axis=0, tiled=True)  15.1 us
    pallas_call x1, Pallas kernels, attend(): pl.pallas_call(attend_kernel, out_shape=pltpu.VMEM((chunks, piece, HD), f...  13.4 us
    all_to_all x1, starting transfers between devices, shards(): back = lax.all_to_all(out, both, split_axis=0, concat_axis=0, tiled=True)  5.5 us
    ppermute x1, waiting for transfers between devices, shards(): second = lax.ppermute(first, 'span', [(0, 1), (1, 0), (2, 3), (3, 2)])  2.65 us
    pallas_call x1, Pallas kernels, prepare(): pl.pallas_call(prepare_kernel, out_shape=(pltpu.VMEM((tokens, HD), incomi...  2.02 us
  transfers between devices with their start and end apart: 2, of which 2 were waited for; matrix products, arithmetic and copies ran while one was open for 1% of the time, Pallas kernels for 2%

profile of v1, /device:TPU:0, one launch (start us, length us, event | category | flops | bytes accessed | tf_op | source)
XLA Modules:
  0.0 97.4 jit_solution(16951804609052632947)
XLA Ops:
  0.0 1.7 %pack.1 = bf16[4,32,96,128]{3,2,1,0:T(8,128)(2,1)S(1)} custom-call(s32[1]{0:T(128)} %bitcast.3.turn_ref, bf16[72,4096]{1,0:T(8,128)(2,1)} %bitcast.16, bf16[72,4096]{1,0:T(8,128)(2,1)} %bitcast.17, bf16[72,4096]{1,0:T(8,128)(2,1)} %bitcast.18), custom_call_target="tpu_custom_call" | custom-call | tf_op jit(solution)/shard_map/pack/pallas_call | solution.py:65
  1.7 52.4 %all_to_all.10.incoming_ref = bf16[128,96,128]{2,1,0:T(8,128)(2,1)S(1)} all-to-all(bf16[128,96,128]{2,1,0:T(8,128)(2,1)S(1)} %bitcast.14), channel_id=1, replica_groups=mesh['span'=4,'ctx'=32] {'span','ctx'}, dimensions={0} | all-to-all | bytes 6291456 | tf_op jit(solution)/shard_map/all_to_all | solution.py:314
  54.2 0.0 copy-start
  54.2 0.0 copy-start.1
  54.2 0.0 copy-start.2
  54.2 1.6 %slice.4 = bf16[128,72,128]{2,1,0:T(8,128)(2,1)} slice(bf16[128,96,128]{2,1,0:T(8,128)(2,1)S(1)} %all_to_all.10.incoming_ref), slice={[0:128], [0:72], [0:128]} | slice | bytes 4718592 | tf_op jit(solution)/shard_map/slice | solution.py:316
  55.7 0.0 collective-permute-start
  55.8 0.0 copy-done
  55.8 0.0 copy-done.1
  55.8 0.1 pad_add_fusion.meta
  55.9 0.0 copy-done.2
  56.0 2.0 %prepare.1 = (bf16[2304,128]{1,0:T(8,128)(2,1)S(1)}, s32[512]{0:T(512)S(1)}) custom-call(s32[10]{0:T(128)S(1)} %pad_add_fusion.meta, bf16[128,96,128]{2,1,0:T(8,128)(2,1)S(1)} %all_to_all.10.incoming_ref), custom_call_target="tpu_custom_call" | custom-call | tf_op jit(solution)/shard_map/prepare/pallas_call | solution.py:135
  58.0 2.6 %collective-permute-done.second_ref = bf16[9216,128]{1,0:T(8,128)(2,1)} collective-permute-done((bf16[9216,128]{1,0:T(8,128)(2,1)}, bf16[9216,128]{1,0:T(8,128)(2,1)}, u32[]{:S(2)}, u32[]{:S(2)}) %collective-permute-start) | collective-permute-done | bytes 2359328 | tf_op jit(solution)/shard_map/ppermute | solution.py:317
  60.6 13.4 %attend.1 = bf16[128,24,128]{2,1,0:T(8,128)(2,1)} custom-call(s32[10]{0:T(128)S(1)} %pad_add_fusion.meta, f32[4]{0:T(128)S(1)} %multiply_add_fusion.gates, s32[512]{0:T(512)S(1)} %get-tuple-element.7.items, bf16[9216,128]{1,0:T(8,128)(2,1)} %bitcast.8.first_ref, bf16[9216,128]{1,0:T(8,128)(2,1)} %collective-permute-done.second_ref, ...), custom_call_target="tpu_custom_call" | custom-call | tf_op jit(solution)/shard_map/attend/pallas_call | solution.py:276
  74.1 5.5 %all-to-all-start.1 = ((bf16[128,24,128]{2,1,0:T(8,128)(2,1)}), bf16[128,24,128]{2,1,0:T(8,128)(2,1)S(1)}, u32[]{:S(2)}, u32[]{:S(2)}) async-start(bf16[128,24,128]{2,1,0:T(8,128)(2,1)} %attend.1), calls=%async_computation.1 | async-start | bytes 1572864 | tf_op jit(solution)/shard_map/all_to_all | solution.py:322
  79.6 0.6 dynamic_slice.6
  80.2 0.7 add_compare_fusion
  80.8 15.1 %all-to-all-done.1 = bf16[128,24,128]{2,1,0:T(8,128)(2,1)S(1)} async-done(((bf16[128,24,128]{2,1,0:T(8,128)(2,1)}), bf16[128,24,128]{2,1,0:T(8,128)(2,1)S(1)}, u32[]{:S(2)}, u32[]{:S(2)}) %all-to-all-start.1) | async-done | bytes 786464 | tf_op jit(solution)/shard_map/all_to_all | solution.py:322
  95.9 0.2 fusion.1
  96.2 0.1 copy.7
  96.3 0.3 reshape.49
  96.5 0.9 broadcast_select_fusion
  (1 shorter events, 0.0 us)
Async XLA Ops:
  54.2 1.7 %copy-start = (s32[4]{0:T(128)S(1)}, s32[4]{0:T(128)}, u32[]{:S(2)}) copy-start(s32[4]{0:T(128)} %param.10) | copy-start | bytes 52
  54.2 1.7 %copy-start.1 = (s32[4]{0:T(128)S(1)}, s32[4]{0:T(128)}, u32[]{:S(2)}) copy-start(s32[4]{0:T(128)} %param.11) | copy-start | bytes 52
  54.2 1.7 %copy-start.2 = (s32[4]{0:T(128)S(1)}, s32[4]{0:T(128)}, u32[]{:S(2)}) copy-start(s32[4]{0:T(128)} %param.9) | copy-start | bytes 52
  55.7 4.9 %collective-permute-start = (bf16[9216,128]{1,0:T(8,128)(2,1)}, bf16[9216,128]{1,0:T(8,128)(2,1)}, u32[]{:S(2)}, u32[]{:S(2)}) collective-permute-start(bf16[9216,128]{1,0:T(8,128)(2,1)} %bitcast.8.first_ref), channel_id=1, source_target_pairs={{0,32},{32,0},{64,96},{96,64},{1,33},{33,1},{65,97},{97,65},{2,34}... | collective-permute-start | bytes 7077896 | tf_op jit(solution)/shard_map/ppermute | solution.py:317
  74.1 21.9 %all-to-all-start.1 = ((bf16[128,24,128]{2,1,0:T(8,128)(2,1)}), bf16[128,24,128]{2,1,0:T(8,128)(2,1)S(1)}, u32[]{:S(2)}, u32[]{:S(2)}) async-start(bf16[128,24,128]{2,1,0:T(8,128)(2,1)} %attend.1), calls=%async_computation.1 | async-start | bytes 1572864 | tf_op jit(solution)/shard_map/all_to_all | solution.py:322

commit v2 on v1

--- a/solution.py
+++ b/solution.py
@@ -14,10 +14,10 @@
 KEY_BLOCK = 768
 EDGE_ROWS = 128
 QUERY_TILE = 144
-GROUP = 4
+GROUP = 6
 PACK_HEADS = 8
 ITEMS = 512
-ATTEND_VMEM = 24 * 1024 * 1024
+ATTEND_VMEM = 28 * 1024 * 1024
 PREPARE_VMEM = 8 * 1024 * 1024
 
 
@@ -87,9 +87,7 @@
         return tile + (block << 8) + (span << 16) + (flag << 20)
 
     idle = item(SPANS * span_tiles, 0, 0, 1)
-    at = jnp.int32(GROUP)
-    for extra in range(GROUP):
-        items[extra] = idle
+    at = jnp.int32(0)
     per_tile = SPANS * QUERY_TILE
     span_blocks = tokens // KEY_BLOCK
     blocks = [(meta[SPANS + e] + KEY_BLOCK - 1) // KEY_BLOCK for e in range(SPANS)]
@@ -235,24 +233,38 @@
 
     acc[...] = jnp.ones(acc.shape, acc.dtype)
     top[...] = jnp.zeros(top.shape, top.dtype)
-    for g in range(GROUP):
-        weights[g][...] = jnp.ones(weights[g].shape, weights[g].dtype)
-        scales[g][...] = jnp.zeros(scales[g].shape, scales[g].dtype)
-        score(GROUP + g, GROUP + g)
+
+    def group(step, first, at):
+        for g in range(GROUP):
+            step(first + g, at + g)
+
+    group(score, 0, 0)
+    group(score, GROUP, GROUP)
+    group(weigh, 0, 0)
 
     def two_steps(j, carry):
-        for half in range(2):
-            here, there = (half + 1) % 2 * GROUP, half * GROUP
-            first = (2 * j + half) * GROUP
-            for g in range(GROUP):
-                score(first + 2 * GROUP + g, there + g)
-            for g in range(GROUP):
-                weigh(first + GROUP + g, here + g)
-            for g in range(GROUP):
-                mix(first + g, there + g)
+        first = 2 * j * GROUP
+        group(score, first + 2 * GROUP, 0)
+        group(weigh, first + GROUP, GROUP)
+        group(mix, first, 0)
+        group(score, first + 3 * GROUP, GROUP)
+        group(weigh, first + 2 * GROUP, 0)
+        group(mix, first + GROUP, GROUP)
         return carry
 
-    lax.fori_loop(0, (items[ITEMS - 1] + 2 * GROUP - 1) // (2 * GROUP), two_steps, 0)
+    count = items[ITEMS - 1]
+    pairs = count // (2 * GROUP)
+    lax.fori_loop(0, pairs, two_steps, 0)
+    done = pairs * 2 * GROUP
+
+    @pl.when(done < count)
+    def _():
+        group(mix, done, 0)
+
+    @pl.when(done + GROUP < count)
+    def _():
+        group(weigh, done + GROUP, GROUP)
+        group(mix, done + GROUP, GROUP)
 
     def hand_back(t, carry):
         for k in range(3):
@@ -260,7 +272,7 @@
             o_ref[t * SPANS + (member + 1 + k) % SPANS] = results[rows, :].astype(o_ref.dtype)
         return carry
 
-    lax.fori_loop(0, chunks // SPANS, hand_back, 0)
+    lax.fori_loop(0, chunks // SPANS, hand_back, 0, unroll=4)
 
 
 def attend(first, second, incoming, meta, gates):

time: 99.2 us -> 104 us (1.048); the launches traced: 97.4 us -> 104 us
  Pallas kernels: 17.2 us -> 23.9 us
    pallas_call x1, Pallas kernels: 13.4 us -> 19.8 us  [attend(): pl.pallas_call(attend_kernel, out_shape=pltpu.VMEM((chunks, piece, HD), f...]
where the time goes in v2:
time: 104 us
  blocking collectives  52.4 us (50%)
  Pallas kernels  23.9 us (23%)
  waiting for transfers between devices  17.4 us (17%)
  starting transfers between devices  5.52 us (5%)
  local copies, waits for them, and re-layouts  2.53 us (2%)
  other arithmetic  1.91 us (2%)
    all_to_all x1, blocking collectives, shards(): lax.all_to_all(outgoing, both, split_axis=0, concat_axis=0, tiled=True)  52.4 us
    pallas_call x1, Pallas kernels, attend(): pl.pallas_call(attend_kernel, out_shape=pltpu.VMEM((chunks, piece, HD), f...  19.8 us
    all_to_all x1, waiting for transfers between devices, shards(): back = lax.all_to_all(out, both, split_axis=0, concat_axis=0, tiled=True)  15.1 us
    all_to_all x1, starting transfers between devices, shards(): back = lax.all_to_all(out, both, split_axis=0, concat_axis=0, tiled=True)  5.51 us
    pallas_call x1, Pallas kernels, prepare(): pl.pallas_call(prepare_kernel, out_shape=(pltpu.VMEM((tokens, HD), incomi...  2.38 us
    ppermute x1, waiting for transfers between devices, shards(): second = lax.ppermute(first, 'span', [(0, 1), (1, 0), (2, 3), (3, 2)])  2.28 us
  transfers between devices with their start and end apart: 2, of which 2 were waited for; matrix products, arithmetic and copies ran while one was open for 1% of the time, Pallas kernels for 2%

profile of v2, /device:TPU:0, one launch (start us, length us, event | category | flops | bytes accessed | tf_op | source)
XLA Modules:
  0.0 103.8 jit_solution(12847389225155949412)
XLA Ops:
  0.0 1.7 %pack.1 = bf16[4,32,96,128]{3,2,1,0:T(8,128)(2,1)S(1)} custom-call(s32[1]{0:T(128)} %bitcast.3.turn_ref, bf16[72,4096]{1,0:T(8,128)(2,1)} %bitcast.16, bf16[72,4096]{1,0:T(8,128)(2,1)} %bitcast.17, bf16[72,4096]{1,0:T(8,128)(2,1)} %bitcast.18), custom_call_target="tpu_custom_call" | custom-call | tf_op jit(solution)/shard_map/pack/pallas_call | solution.py:65
  1.7 52.4 %all_to_all.10.incoming_ref = bf16[128,96,128]{2,1,0:T(8,128)(2,1)S(1)} all-to-all(bf16[128,96,128]{2,1,0:T(8,128)(2,1)S(1)} %bitcast.14), channel_id=1, replica_groups=mesh['span'=4,'ctx'=32] {'span','ctx'}, dimensions={0} | all-to-all | bytes 6291456 | tf_op jit(solution)/shard_map/all_to_all | solution.py:326
  54.2 0.0 copy-start
  54.2 0.0 copy-start.1
  54.2 0.0 copy-start.2
  54.2 1.6 %slice.4 = bf16[128,72,128]{2,1,0:T(8,128)(2,1)} slice(bf16[128,96,128]{2,1,0:T(8,128)(2,1)S(1)} %all_to_all.10.incoming_ref), slice={[0:128], [0:72], [0:128]} | slice | bytes 4718592 | tf_op jit(solution)/shard_map/slice | solution.py:328
  55.7 0.0 collective-permute-start
  55.8 0.0 copy-done
  55.8 0.0 copy-done.1
  55.8 0.1 pad_add_fusion.meta
  55.9 0.0 copy-done.2
  56.0 2.4 %prepare.1 = (bf16[2304,128]{1,0:T(8,128)(2,1)S(1)}, s32[512]{0:T(512)S(1)}) custom-call(s32[10]{0:T(128)S(1)} %pad_add_fusion.meta, bf16[128,96,128]{2,1,0:T(8,128)(2,1)S(1)} %all_to_all.10.incoming_ref), custom_call_target="tpu_custom_call" | custom-call | tf_op jit(solution)/shard_map/prepare/pallas_call | solution.py:133
  58.3 2.3 %collective-permute-done.second_ref = bf16[9216,128]{1,0:T(8,128)(2,1)} collective-permute-done((bf16[9216,128]{1,0:T(8,128)(2,1)}, bf16[9216,128]{1,0:T(8,128)(2,1)}, u32[]{:S(2)}, u32[]{:S(2)}) %collective-permute-start) | collective-permute-done | bytes 2359328 | tf_op jit(solution)/shard_map/ppermute | solution.py:329
  60.6 19.8 %attend.1 = bf16[128,24,128]{2,1,0:T(8,128)(2,1)} custom-call(s32[10]{0:T(128)S(1)} %pad_add_fusion.meta, f32[4]{0:T(128)S(1)} %multiply_add_fusion.gates, s32[512]{0:T(512)S(1)} %get-tuple-element.7.items, bf16[9216,128]{1,0:T(8,128)(2,1)} %bitcast.8.first_ref, bf16[9216,128]{1,0:T(8,128)(2,1)} %collective-permute-done.second_ref, ...), custom_call_target="tpu_custom_call" | custom-call | tf_op jit(solution)/shard_map/attend/pallas_call | solution.py:288
  80.4 5.5 %all-to-all-start.1 = ((bf16[128,24,128]{2,1,0:T(8,128)(2,1)}), bf16[128,24,128]{2,1,0:T(8,128)(2,1)S(1)}, u32[]{:S(2)}, u32[]{:S(2)}) async-start(bf16[128,24,128]{2,1,0:T(8,128)(2,1)} %attend.1), calls=%async_computation.1 | async-start | bytes 1572864 | tf_op jit(solution)/shard_map/all_to_all | solution.py:334
  86.0 0.6 dynamic_slice.6
  86.6 0.7 add_compare_fusion
  87.2 15.1 %all-to-all-done.1 = bf16[128,24,128]{2,1,0:T(8,128)(2,1)S(1)} async-done(((bf16[128,24,128]{2,1,0:T(8,128)(2,1)}), bf16[128,24,128]{2,1,0:T(8,128)(2,1)S(1)}, u32[]{:S(2)}, u32[]{:S(2)}) %all-to-all-start.1) | async-done | bytes 786464 | tf_op jit(solution)/shard_map/all_to_all | solution.py:334
  102.3 0.2 fusion.1
  102.5 0.1 copy.7
  102.6 0.3 reshape.49
  102.9 0.9 broadcast_select_fusion
  (1 shorter events, 0.0 us)
Async XLA Ops:
  54.2 1.7 %copy-start = (s32[4]{0:T(128)S(1)}, s32[4]{0:T(128)}, u32[]{:S(2)}) copy-start(s32[4]{0:T(128)} %param.10) | copy-start | bytes 52
  54.2 1.7 %copy-start.1 = (s32[4]{0:T(128)S(1)}, s32[4]{0:T(128)}, u32[]{:S(2)}) copy-start(s32[4]{0:T(128)} %param.11) | copy-start | bytes 52
  54.2 1.7 %copy-start.2 = (s32[4]{0:T(128)S(1)}, s32[4]{0:T(128)}, u32[]{:S(2)}) copy-start(s32[4]{0:T(128)} %param.9) | copy-start | bytes 52
  55.7 4.9 %collective-permute-start = (bf16[9216,128]{1,0:T(8,128)(2,1)}, bf16[9216,128]{1,0:T(8,128)(2,1)}, u32[]{:S(2)}, u32[]{:S(2)}) collective-permute-start(bf16[9216,128]{1,0:T(8,128)(2,1)} %bitcast.8.first_ref), channel_id=1, source_target_pairs={{0,32},{32,0},{64,96},{96,64},{1,33},{33,1},{65,97},{97,65},{2,34}... | collective-permute-start | bytes 7077896 | tf_op jit(solution)/shard_map/ppermute | solution.py:329
  80.4 21.9 %all-to-all-start.1 = ((bf16[128,24,128]{2,1,0:T(8,128)(2,1)}), bf16[128,24,128]{2,1,0:T(8,128)(2,1)S(1)}, u32[]{:S(2)}, u32[]{:S(2)}) async-start(bf16[128,24,128]{2,1,0:T(8,128)(2,1)} %attend.1), calls=%async_computation.1 | async-start | bytes 1572864 | tf_op jit(solution)/shard_map/all_to_all | solution.py:334

commit v3 on v2

--- a/solution.py
+++ b/solution.py
@@ -147,7 +147,7 @@
     meta, gates, items, first_ref, second_ref, queries, o_ref,
     keys, values, scores, highs, weights, scales, acc, top, results, sems,
 ):
-    chunks, piece = o_ref.shape[0], o_ref.shape[1]
+    piece = o_ref.shape[1]
     tokens = first_ref.shape[0] // SPANS
     all_tiles = tokens // QUERY_TILE
     core, member = meta[2 * SPANS], meta[2 * SPANS + 1]
@@ -195,7 +195,15 @@
                 values[rows, columns] = jnp.where(valid, mixed, 0.0).astype(values.dtype)
             return carry
 
-        lax.fori_loop(count // EDGE_ROWS, ends, edge, 0)
+        def fill(s, carry, e=e, first_key=first_key):
+            rows = pl.ds(pl.multiple_of(e * tokens + s * EDGE_ROWS, EDGE_ROWS), EDGE_ROWS)
+            keys[rows, :] = jnp.broadcast_to(first_key, (EDGE_ROWS, HD)).astype(keys.dtype)
+            values[rows, :] = jnp.zeros((EDGE_ROWS, 2 * HD), values.dtype)
+            return carry
+
+        full = (count + EDGE_ROWS - 1) // EDGE_ROWS
+        lax.fori_loop(count // EDGE_ROWS, full, edge, 0)
+        lax.fori_loop(full, ends, fill, 0)
 
     def key_rows(i):
         return pl.ds(pl.multiple_of((items[i] >> 8 & 255) * KEY_BLOCK, KEY_BLOCK), KEY_BLOCK)
@@ -257,22 +265,30 @@
     lax.fori_loop(0, pairs, two_steps, 0)
     done = pairs * 2 * GROUP
 
-    @pl.when(done < count)
+    @pl.when((done < count) & (done + GROUP >= count))
     def _():
         group(mix, done, 0)
 
     @pl.when(done + GROUP < count)
     def _():
         group(weigh, done + GROUP, GROUP)
+        group(mix, done, 0)
         group(mix, done + GROUP, GROUP)
 
-    def hand_back(t, carry):
-        for k in range(3):
-            rows = pl.ds(pl.multiple_of((t * 3 + k) * piece, 8), piece)
-            o_ref[t * SPANS + (member + 1 + k) % SPANS] = results[rows, :].astype(o_ref.dtype)
-        return carry
-
-    lax.fori_loop(0, chunks // SPANS, hand_back, 0, unroll=4)
+    per_load = QUERY_TILE // (3 * piece)
+    for c in range(SPANS):
+
+        def hand_back(t, carry, c=c):
+            for n in range(per_load):
+                group_of = (c * all_tiles // SPANS + t) * per_load + n
+                for k in range(3):
+                    rows = pl.ds(pl.multiple_of((group_of * 3 + k) * piece, 8), piece)
+                    source = group_of * SPANS + (member + 1 + k) % SPANS
+                    o_ref[source] = results[rows, :].astype(o_ref.dtype)
+            return carry
+
+        per_tile = SPANS * QUERY_TILE
+        lax.fori_loop(0, (meta[SPANS + c] + per_tile - 1) // per_tile, hand_back, 0)
 
 
 def attend(first, second, incoming, meta, gates):

time: 104 us -> 102 us (0.981); the launches traced: 104 us -> 100 us
  Pallas kernels: 23.9 us -> 20.2 us
    pallas_call x1, Pallas kernels: 19.8 us -> 16.3 us  [attend(): pl.pallas_call(attend_kernel, out_shape=pltpu.VMEM((chunks, piece, HD), f...]
where the time goes in v3:
time: 102 us; the launch traced here: 100 us
  blocking collectives  52.4 us (51%)
  Pallas kernels  20.2 us (20%)
  waiting for transfers between devices  17.6 us (17%)
  starting transfers between devices  5.5 us (5%)
  local copies, waits for them, and re-layouts  2.53 us (2%)
  other arithmetic  1.91 us (2%)
    all_to_all x1, blocking collectives, shards(): lax.all_to_all(outgoing, both, split_axis=0, concat_axis=0, tiled=True)  52.4 us
    pallas_call x1, Pallas kernels, attend(): pl.pallas_call(attend_kernel, out_shape=pltpu.VMEM((chunks, piece, HD), f...  16.3 us
    all_to_all x1, waiting for transfers between devices, shards(): back = lax.all_to_all(out, both, split_axis=0, concat_axis=0, tiled=True)  15.1 us
    all_to_all x1, starting transfers between devices, shards(): back = lax.all_to_all(out, both, split_axis=0, concat_axis=0, tiled=True)  5.5 us
    ppermute x1, waiting for transfers between devices, shards(): second = lax.ppermute(first, 'span', [(0, 1), (1, 0), (2, 3), (3, 2)])  2.48 us
    pallas_call x1, Pallas kernels, prepare(): pl.pallas_call(prepare_kernel, out_shape=(pltpu.VMEM((tokens, HD), incomi...  2.18 us
  transfers between devices with their start and end apart: 2, of which 2 were waited for; matrix products, arithmetic and copies ran while one was open for 1% of the time, Pallas kernels for 2%

profile of v3, /device:TPU:0, one launch (start us, length us, event | category | flops | bytes accessed | tf_op | source)
XLA Modules:
  0.0 100.3 jit_solution(3971285195628631773)
XLA Ops:
  0.0 1.7 %pack.1 = bf16[4,32,96,128]{3,2,1,0:T(8,128)(2,1)S(1)} custom-call(s32[1]{0:T(128)} %bitcast.3.turn_ref, bf16[72,4096]{1,0:T(8,128)(2,1)} %bitcast.16, bf16[72,4096]{1,0:T(8,128)(2,1)} %bitcast.17, bf16[72,4096]{1,0:T(8,128)(2,1)} %bitcast.18), custom_call_target="tpu_custom_call" | custom-call | tf_op jit(solution)/shard_map/pack/pallas_call | solution.py:65
  1.7 52.4 %all_to_all.10.incoming_ref = bf16[128,96,128]{2,1,0:T(8,128)(2,1)S(1)} all-to-all(bf16[128,96,128]{2,1,0:T(8,128)(2,1)S(1)} %bitcast.14), channel_id=1, replica_groups=mesh['span'=4,'ctx'=32] {'span','ctx'}, dimensions={0} | all-to-all | bytes 6291456 | tf_op jit(solution)/shard_map/all_to_all | solution.py:342
  54.2 0.0 copy-start
  54.2 0.0 copy-start.1
  54.2 0.0 copy-start.2
  54.2 1.6 %slice.4 = bf16[128,72,128]{2,1,0:T(8,128)(2,1)} slice(bf16[128,96,128]{2,1,0:T(8,128)(2,1)S(1)} %all_to_all.10.incoming_ref), slice={[0:128], [0:72], [0:128]} | slice | bytes 4718592 | tf_op jit(solution)/shard_map/slice | solution.py:344
  55.7 0.0 collective-permute-start
  55.8 0.0 copy-done
  55.8 0.0 copy-done.1
  55.8 0.1 pad_add_fusion.meta
  55.9 0.0 copy-done.2
  56.0 2.2 %prepare.1 = (bf16[2304,128]{1,0:T(8,128)(2,1)S(1)}, s32[512]{0:T(512)S(1)}) custom-call(s32[10]{0:T(128)S(1)} %pad_add_fusion.meta, bf16[128,96,128]{2,1,0:T(8,128)(2,1)S(1)} %all_to_all.10.incoming_ref), custom_call_target="tpu_custom_call" | custom-call | tf_op jit(solution)/shard_map/prepare/pallas_call | solution.py:133
  58.1 2.5 %collective-permute-done.second_ref = bf16[9216,128]{1,0:T(8,128)(2,1)} collective-permute-done((bf16[9216,128]{1,0:T(8,128)(2,1)}, bf16[9216,128]{1,0:T(8,128)(2,1)}, u32[]{:S(2)}, u32[]{:S(2)}) %collective-permute-start) | collective-permute-done | bytes 2359328 | tf_op jit(solution)/shard_map/ppermute | solution.py:345
  60.6 16.3 %attend.1 = bf16[128,24,128]{2,1,0:T(8,128)(2,1)} custom-call(s32[10]{0:T(128)S(1)} %pad_add_fusion.meta, f32[4]{0:T(128)S(1)} %multiply_add_fusion.gates, s32[512]{0:T(512)S(1)} %get-tuple-element.7.items, bf16[9216,128]{1,0:T(8,128)(2,1)} %bitcast.8.first_ref, bf16[9216,128]{1,0:T(8,128)(2,1)} %collective-permute-done.second_ref, ...), custom_call_target="tpu_custom_call" | custom-call | tf_op jit(solution)/shard_map/attend/pallas_call | solution.py:304
  76.9 5.5 %all-to-all-start.1 = ((bf16[128,24,128]{2,1,0:T(8,128)(2,1)}), bf16[128,24,128]{2,1,0:T(8,128)(2,1)S(1)}, u32[]{:S(2)}, u32[]{:S(2)}) async-start(bf16[128,24,128]{2,1,0:T(8,128)(2,1)} %attend.1), calls=%async_computation.1 | async-start | bytes 1572864 | tf_op jit(solution)/shard_map/all_to_all | solution.py:350
  82.4 0.6 dynamic_slice.6
  83.0 0.7 add_compare_fusion
  83.7 15.1 %all-to-all-done.1 = bf16[128,24,128]{2,1,0:T(8,128)(2,1)S(1)} async-done(((bf16[128,24,128]{2,1,0:T(8,128)(2,1)}), bf16[128,24,128]{2,1,0:T(8,128)(2,1)S(1)}, u32[]{:S(2)}, u32[]{:S(2)}) %all-to-all-start.1) | async-done | bytes 786464 | tf_op jit(solution)/shard_map/all_to_all | solution.py:350
  98.8 0.2 fusion.1
  99.0 0.1 copy.7
  99.1 0.3 reshape.49
  99.3 0.9 broadcast_select_fusion
  (1 shorter events, 0.0 us)
Async XLA Ops:
  54.2 1.7 %copy-start = (s32[4]{0:T(128)S(1)}, s32[4]{0:T(128)}, u32[]{:S(2)}) copy-start(s32[4]{0:T(128)} %param.10) | copy-start | bytes 52
  54.2 1.7 %copy-start.1 = (s32[4]{0:T(128)S(1)}, s32[4]{0:T(128)}, u32[]{:S(2)}) copy-start(s32[4]{0:T(128)} %param.11) | copy-start | bytes 52
  54.2 1.7 %copy-start.2 = (s32[4]{0:T(128)S(1)}, s32[4]{0:T(128)}, u32[]{:S(2)}) copy-start(s32[4]{0:T(128)} %param.9) | copy-start | bytes 52
  55.7 4.9 %collective-permute-start = (bf16[9216,128]{1,0:T(8,128)(2,1)}, bf16[9216,128]{1,0:T(8,128)(2,1)}, u32[]{:S(2)}, u32[]{:S(2)}) collective-permute-start(bf16[9216,128]{1,0:T(8,128)(2,1)} %bitcast.8.first_ref), channel_id=1, source_target_pairs={{0,32},{32,0},{64,96},{96,64},{1,33},{33,1},{65,97},{97,65},{2,34}... | collective-permute-start | bytes 7077896 | tf_op jit(solution)/shard_map/ppermute | solution.py:345
  76.9 21.9 %all-to-all-start.1 = ((bf16[128,24,128]{2,1,0:T(8,128)(2,1)}), bf16[128,24,128]{2,1,0:T(8,128)(2,1)S(1)}, u32[]{:S(2)}, u32[]{:S(2)}) async-start(bf16[128,24,128]{2,1,0:T(8,128)(2,1)} %attend.1), calls=%async_computation.1 | async-start | bytes 1572864 | tf_op jit(solution)/shard_map/all_to_all | solution.py:350

commit v4 on v3

--- a/solution.py
+++ b/solution.py
@@ -14,7 +14,7 @@
 KEY_BLOCK = 768
 EDGE_ROWS = 128
 QUERY_TILE = 144
-GROUP = 6
+GROUP = 5
 PACK_HEADS = 8
 ITEMS = 512
 ATTEND_VMEM = 28 * 1024 * 1024

time: 102 us -> 101 us (level); the launches traced: 100 us -> 102 us
  Pallas kernels: 20.2 us -> 22.2 us
    pallas_call x1, Pallas kernels: 16.3 us -> 18.2 us  [attend(): pl.pallas_call(attend_kernel, out_shape=pltpu.VMEM((chunks, piece, HD), f...]
where the time goes in v4:
time: 101 us; the launch traced here: 102 us
  blocking collectives  52.4 us (52%)
  Pallas kernels  22.2 us (22%)
  waiting for transfers between devices  17.5 us (17%)
  starting transfers between devices  5.51 us (5%)
  local copies, waits for them, and re-layouts  2.53 us (3%)
  other arithmetic  1.91 us (2%)
    all_to_all x1, blocking collectives, shards(): lax.all_to_all(outgoing, both, split_axis=0, concat_axis=0, tiled=True)  52.4 us
    pallas_call x1, Pallas kernels, attend(): pl.pallas_call(attend_kernel, out_shape=pltpu.VMEM((chunks, piece, HD), f...  18.2 us
    all_to_all x1, waiting for transfers between devices, shards(): back = lax.all_to_all(out, both, split_axis=0, concat_axis=0, tiled=True)  15.1 us
    all_to_all x1, starting transfers between devices, shards(): back = lax.all_to_all(out, both, split_axis=0, concat_axis=0, tiled=True)  5.5 us
    ppermute x1, waiting for transfers between devices, shards(): second = lax.ppermute(first, 'span', [(0, 1), (1, 0), (2, 3), (3, 2)])  2.4 us
    pallas_call x1, Pallas kernels, prepare(): pl.pallas_call(prepare_kernel, out_shape=(pltpu.VMEM((tokens, HD), incomi...  2.27 us
  transfers between devices with their start and end apart: 2, of which 2 were waited for; matrix products, arithmetic and copies ran while one was open for 1% of the time, Pallas kernels for 2%

profile of v4, /device:TPU:0, one launch (start us, length us, event | category | flops | bytes accessed | tf_op | source)
XLA Modules:
  0.0 102.2 jit_solution(11050633225166246746)
XLA Ops:
  0.0 1.7 %pack.1 = bf16[4,32,96,128]{3,2,1,0:T(8,128)(2,1)S(1)} custom-call(s32[1]{0:T(128)} %bitcast.3.turn_ref, bf16[72,4096]{1,0:T(8,128)(2,1)} %bitcast.16, bf16[72,4096]{1,0:T(8,128)(2,1)} %bitcast.17, bf16[72,4096]{1,0:T(8,128)(2,1)} %bitcast.18), custom_call_target="tpu_custom_call" | custom-call | tf_op jit(solution)/shard_map/pack/pallas_call | solution.py:65
  1.7 52.4 %all_to_all.10.incoming_ref = bf16[128,96,128]{2,1,0:T(8,128)(2,1)S(1)} all-to-all(bf16[128,96,128]{2,1,0:T(8,128)(2,1)S(1)} %bitcast.14), channel_id=1, replica_groups=mesh['span'=4,'ctx'=32] {'span','ctx'}, dimensions={0} | all-to-all | bytes 6291456 | tf_op jit(solution)/shard_map/all_to_all | solution.py:342
  54.2 0.0 copy-start
  54.2 0.0 copy-start.1
  54.2 0.0 copy-start.2
  54.2 1.6 %slice.4 = bf16[128,72,128]{2,1,0:T(8,128)(2,1)} slice(bf16[128,96,128]{2,1,0:T(8,128)(2,1)S(1)} %all_to_all.10.incoming_ref), slice={[0:128], [0:72], [0:128]} | slice | bytes 4718592 | tf_op jit(solution)/shard_map/slice | solution.py:344
  55.7 0.0 collective-permute-start
  55.8 0.0 copy-done
  55.8 0.0 copy-done.1
  55.8 0.1 pad_add_fusion.meta
  55.9 0.0 copy-done.2
  56.0 2.3 %prepare.1 = (bf16[2304,128]{1,0:T(8,128)(2,1)S(1)}, s32[512]{0:T(512)S(1)}) custom-call(s32[10]{0:T(128)S(1)} %pad_add_fusion.meta, bf16[128,96,128]{2,1,0:T(8,128)(2,1)S(1)} %all_to_all.10.incoming_ref), custom_call_target="tpu_custom_call" | custom-call | tf_op jit(solution)/shard_map/prepare/pallas_call | solution.py:133
  58.2 2.4 %collective-permute-done.second_ref = bf16[9216,128]{1,0:T(8,128)(2,1)} collective-permute-done((bf16[9216,128]{1,0:T(8,128)(2,1)}, bf16[9216,128]{1,0:T(8,128)(2,1)}, u32[]{:S(2)}, u32[]{:S(2)}) %collective-permute-start) | collective-permute-done | bytes 2359328 | tf_op jit(solution)/shard_map/ppermute | solution.py:345
  60.6 18.2 %attend.1 = bf16[128,24,128]{2,1,0:T(8,128)(2,1)} custom-call(s32[10]{0:T(128)S(1)} %pad_add_fusion.meta, f32[4]{0:T(128)S(1)} %multiply_add_fusion.gates, s32[512]{0:T(512)S(1)} %get-tuple-element.7.items, bf16[9216,128]{1,0:T(8,128)(2,1)} %bitcast.8.first_ref, bf16[9216,128]{1,0:T(8,128)(2,1)} %collective-permute-done.second_ref, ...), custom_call_target="tpu_custom_call" | custom-call | tf_op jit(solution)/shard_map/attend/pallas_call | solution.py:304
  78.8 5.5 %all-to-all-start.1 = ((bf16[128,24,128]{2,1,0:T(8,128)(2,1)}), bf16[128,24,128]{2,1,0:T(8,128)(2,1)S(1)}, u32[]{:S(2)}, u32[]{:S(2)}) async-start(bf16[128,24,128]{2,1,0:T(8,128)(2,1)} %attend.1), calls=%async_computation.1 | async-start | bytes 1572864 | tf_op jit(solution)/shard_map/all_to_all | solution.py:350
  84.4 0.6 dynamic_slice.6
  84.9 0.7 add_compare_fusion
  85.6 15.1 %all-to-all-done.1 = bf16[128,24,128]{2,1,0:T(8,128)(2,1)S(1)} async-done(((bf16[128,24,128]{2,1,0:T(8,128)(2,1)}), bf16[128,24,128]{2,1,0:T(8,128)(2,1)S(1)}, u32[]{:S(2)}, u32[]{:S(2)}) %all-to-all-start.1) | async-done | bytes 786464 | tf_op jit(solution)/shard_map/all_to_all | solution.py:350
  100.7 0.2 fusion.1
  100.9 0.1 copy.7
  101.0 0.3 reshape.49
  101.3 0.9 broadcast_select_fusion
  (1 shorter events, 0.0 us)
Async XLA Ops:
  54.2 1.7 %copy-start = (s32[4]{0:T(128)S(1)}, s32[4]{0:T(128)}, u32[]{:S(2)}) copy-start(s32[4]{0:T(128)} %param.10) | copy-start | bytes 52
  54.2 1.7 %copy-start.1 = (s32[4]{0:T(128)S(1)}, s32[4]{0:T(128)}, u32[]{:S(2)}) copy-start(s32[4]{0:T(128)} %param.11) | copy-start | bytes 52
  54.2 1.7 %copy-start.2 = (s32[4]{0:T(128)S(1)}, s32[4]{0:T(128)}, u32[]{:S(2)}) copy-start(s32[4]{0:T(128)} %param.9) | copy-start | bytes 52
  55.7 4.9 %collective-permute-start = (bf16[9216,128]{1,0:T(8,128)(2,1)}, bf16[9216,128]{1,0:T(8,128)(2,1)}, u32[]{:S(2)}, u32[]{:S(2)}) collective-permute-start(bf16[9216,128]{1,0:T(8,128)(2,1)} %bitcast.8.first_ref), channel_id=1, source_target_pairs={{0,32},{32,0},{64,96},{96,64},{1,33},{33,1},{65,97},{97,65},{2,34}... | collective-permute-start | bytes 7077896 | tf_op jit(solution)/shard_map/ppermute | solution.py:345
  78.8 21.9 %all-to-all-start.1 = ((bf16[128,24,128]{2,1,0:T(8,128)(2,1)}), bf16[128,24,128]{2,1,0:T(8,128)(2,1)S(1)}, u32[]{:S(2)}, u32[]{:S(2)}) async-start(bf16[128,24,128]{2,1,0:T(8,128)(2,1)} %attend.1), calls=%async_computation.1 | async-start | bytes 1572864 | tf_op jit(solution)/shard_map/all_to_all | solution.py:350
